TPU v7x, 32 devices: a whole 2x2x4 slice. The times are simulated.
32 devices in a mesh: block: 4 (over x, core), tok: 8 (over z, y).
Axes of the slice: x: 2, y: 2, z: 4, core: 2. Of those that a mesh axis runs over, the one named last changes fastest.
Arguments:
- query: bfloat16 [12288, 10, 256], P(('block', 'tok')), may hold values from -6 to 6
- key: bfloat16 [12288, 10, 256], P(('block', 'tok')), may hold values from -6 to 6
- value: bfloat16 [12288, 10, 256], P(('block', 'tok')), may hold values from -6 to 6
- rates: float32 [10, 12288], P(None, ('block', 'tok')), may hold values from 0.01 to 0.3
- init_weights: float32 [10, 3, 256, 256], P(None, None, 'tok'), may hold values from -0.375 to 0.375
Outputs:
- output: bfloat16 [12288, 10, 256], P(('block', 'tok'))
- states: float32 [4, 10, 3, 256, 256], P('block', None, None, 'tok')
All inputs are finite; a program needn't handle non-finite values.
Results may differ from a plain program's by a relative error of at most 0.013.
The roundings to bfloat16 on the way count: a program that leaves them out, or rounds other values in their place, can miss the bound.
Values may be sent and summed in bfloat16 or wider, within the bound.
A program may use at most 64 MiB of HBM per device.

v0:
```python
import math

import jax
import jax.numpy as jnp
from jax import lax
from jax.sharding import PartitionSpec as P


def passed_along(value, axis, steps):
    count = lax.axis_size(axis)
    leading, last = (max(0, -steps), min(count, count - steps))
    return lax.ppermute(value, axis, [(source, source + steps) for source in range(leading, last)])


def across(left, right):
    return lax.dot_general(
        left, right, (((0,), (0,)), ((), ())), preferred_element_type=jnp.float32
    )


def against(left, right):
    return lax.dot_general(
        left, right, (((1,), (1,)), ((), ())), preferred_element_type=jnp.float32
    )


def on_device(query, key, value, rates, init_weights):
    tok_dev = query.shape[0]
    heads = query.shape[1]
    block = tok_dev * lax.axis_size("tok")
    factor_const = 1.0 / math.sqrt(block)
    place = lax.axis_index("block")
    length = lax.axis_size("block")
    ticks = heads + length - 1

    def tick(step, carry):
        arrived, output, states = carry
        head = step - place
        active = (head >= 0) & (head < heads)
        hsafe = jnp.clip(head, 0, heads - 1)
        own = lax.dynamic_index_in_dim(init_weights, hsafe, 0, keepdims=False)
        current = jnp.where(place == 0, own, arrived)
        full = lax.all_gather(current.astype(jnp.bfloat16), "tok", axis=1, tiled=True)
        quer = lax.dynamic_index_in_dim(query, hsafe, 1, keepdims=False)
        keys = lax.dynamic_index_in_dim(key, hsafe, 1, keepdims=False)
        vals = lax.dynamic_index_in_dim(value, hsafe, 1, keepdims=False)
        lrs = lax.dynamic_index_in_dim(rates, hsafe, 0, keepdims=False)

        def forward(rows_in):
            a_val = against(rows_in, full[0])
            b_val = against(rows_in, full[1])
            sig = jax.nn.sigmoid(a_val)
            s_val = a_val * sig
            return (a_val, b_val, sig, s_val, (s_val * b_val).astype(jnp.bfloat16))

        _, _, _, _, hid_q = forward(quer)
        out_rows = jnp.dot(hid_q, full[2], preferred_element_type=jnp.float32).astype(jnp.bfloat16)
        a_val, b_val, sig, s_val, hid_k = forward(keys)
        factor = lrs * factor_const
        g_val = (-(factor[:, None] * vals.astype(jnp.float32))).astype(jnp.bfloat16)
        dhid = against(g_val, full[2])
        dsil = sig * (1.0 + a_val * (1.0 - sig))
        d_a = (dhid * b_val * dsil).astype(jnp.bfloat16)
        d_b = (dhid * s_val).astype(jnp.bfloat16)
        grads = lax.psum_scatter(
            jnp.stack([across(d_a, keys), across(d_b, keys), across(hid_k, g_val)], axis=1),
            "tok",
            scatter_dimension=0,
            tiled=True,
        )
        grads = jnp.transpose(grads, (1, 0, 2))
        upd = current - grads
        ratio = jnp.sqrt(
            (jnp.mean(current * current, axis=-1) + 1e-06) / (jnp.mean(upd * upd, axis=-1) + 1e-06)
        )
        new_w = upd * ratio[..., None]
        output = jnp.where(
            active, lax.dynamic_update_index_in_dim(output, out_rows, hsafe, 1), output
        )
        states = jnp.where(active, lax.dynamic_update_index_in_dim(states, new_w, hsafe, 0), states)
        sent = passed_along(new_w, "block", 1)
        return (sent, output, states)

    start_carry = (
        jnp.zeros(init_weights.shape[1:], jnp.float32),
        jnp.zeros(query.shape, jnp.bfloat16),
        jnp.zeros(init_weights.shape, jnp.float32),
    )
    _, output, states = lax.fori_loop(0, ticks, tick, start_carry)
    return (output, states[None])


def solution(mesh):
    placed = (
        P(("block", "tok"), None, None),
        P(("block", "tok"), None, None),
        P(("block", "tok"), None, None),
        P(None, ("block", "tok")),
        P(None, None, "tok", None),
    )
    return jax.shard_map(
        on_device,
        mesh=mesh,
        in_specs=placed,
        out_specs=(P(("block", "tok"), None, None), P("block", None, None, "tok", None)),
        check_vma=False,
    )
```

profile of v0, /device:TPU:3, one launch (start us, length us, event | category | flops | bytes accessed | tf_op | source)
XLA Modules:
  0.0 1463.5 jit_solution(16517343167364489921)
XLA Ops:
  8.7 1447.3 %while.18 = (s32[]{:T(128)}, f32[3,32,256]{2,1,0:T(8,128)S(1)}, bf16[384,10,256]{2,0,1:T(8,128)(2,1)}, f32[10,3,32,256]{3,2,1,0:T(8,128)S(1)}, pred[]{:T(512)}, ...) while((s32[]{:T(128)}, f32[3,32,256]{2,1,0:T(8,128)S(1)}, ...), condition=%wide.region_4.5_spmd, body=%wide.region_0.4_spmd.sunk | while | flops 457360032 | bytes 14364864 | solution.py:89
  9.6 25.4 %all_gather.9 = bf16[3,256,256]{2,1,0:T(8,128)(2,1)S(1)} all-gather(bf16[3,32,256]{2,1,0:T(8,128)(2,1)S(1)} %get-tuple-element.321), channel_id=1, replica_groups=mesh['block'=4,'tok'=8] {'tok'}, dimensions={1}, use_global_device_ids=true | all-gather | bytes 442368 | tf_op jit(solution)/shard_map/while/body/eval_jaxpr/all_gather | solution.py:43
  45.3 67.4 %reduce-scatter.2.cloned.1.call-done = f32[32,3,256]{2,0,1:T(8,128)} async-done(((f32[256,3,256]{2,0,1:T(8,128)}), f32[32,3,256]{2,0,1:T(8,128)}) %reduce-scatter.2.cloned.1.call-update) | async-done | bytes 98320 | tf_op jit(solution)/shard_map/while/body/eval_jaxpr/reduce_scatter | solution.py:65
  120.7 25.0 %all_gather.9 = bf16[3,256,256]{2,1,0:T(8,128)(2,1)S(1)} all-gather(bf16[3,32,256]{2,1,0:T(8,128)(2,1)S(1)} %get-tuple-element.321), channel_id=1, replica_groups=mesh['block'=4,'tok'=8] {'tok'}, dimensions={1}, use_global_device_ids=true | all-gather | bytes 442368 | tf_op jit(solution)/shard_map/while/body/eval_jaxpr/all_gather | solution.py:43
  155.9 68.2 %reduce-scatter.2.cloned.1.call-done = f32[32,3,256]{2,0,1:T(8,128)} async-done(((f32[256,3,256]{2,0,1:T(8,128)}), f32[32,3,256]{2,0,1:T(8,128)}) %reduce-scatter.2.cloned.1.call-update) | async-done | bytes 98320 | tf_op jit(solution)/shard_map/while/body/eval_jaxpr/reduce_scatter | solution.py:65
  232.1 25.0 %all_gather.9 = bf16[3,256,256]{2,1,0:T(8,128)(2,1)S(1)} all-gather(bf16[3,32,256]{2,1,0:T(8,128)(2,1)S(1)} %get-tuple-element.321), channel_id=1, replica_groups=mesh['block'=4,'tok'=8] {'tok'}, dimensions={1}, use_global_device_ids=true | all-gather | bytes 442368 | tf_op jit(solution)/shard_map/while/body/eval_jaxpr/all_gather | solution.py:43
  267.4 68.1 %reduce-scatter.2.cloned.1.call-done = f32[32,3,256]{2,0,1:T(8,128)} async-done(((f32[256,3,256]{2,0,1:T(8,128)}), f32[32,3,256]{2,0,1:T(8,128)}) %reduce-scatter.2.cloned.1.call-update) | async-done | bytes 98320 | tf_op jit(solution)/shard_map/while/body/eval_jaxpr/reduce_scatter | solution.py:65
  343.4 25.0 %all_gather.9 = bf16[3,256,256]{2,1,0:T(8,128)(2,1)S(1)} all-gather(bf16[3,32,256]{2,1,0:T(8,128)(2,1)S(1)} %get-tuple-element.321), channel_id=1, replica_groups=mesh['block'=4,'tok'=8] {'tok'}, dimensions={1}, use_global_device_ids=true | all-gather | bytes 442368 | tf_op jit(solution)/shard_map/while/body/eval_jaxpr/all_gather | solution.py:43
  378.7 68.1 %reduce-scatter.2.cloned.1.call-done = f32[32,3,256]{2,0,1:T(8,128)} async-done(((f32[256,3,256]{2,0,1:T(8,128)}), f32[32,3,256]{2,0,1:T(8,128)}) %reduce-scatter.2.cloned.1.call-update) | async-done | bytes 98320 | tf_op jit(solution)/shard_map/while/body/eval_jaxpr/reduce_scatter | solution.py:65
  454.7 25.0 %all_gather.9 = bf16[3,256,256]{2,1,0:T(8,128)(2,1)S(1)} all-gather(bf16[3,32,256]{2,1,0:T(8,128)(2,1)S(1)} %get-tuple-element.321), channel_id=1, replica_groups=mesh['block'=4,'tok'=8] {'tok'}, dimensions={1}, use_global_device_ids=true | all-gather | bytes 442368 | tf_op jit(solution)/shard_map/while/body/eval_jaxpr/all_gather | solution.py:43
  490.0 68.2 %reduce-scatter.2.cloned.1.call-done = f32[32,3,256]{2,0,1:T(8,128)} async-done(((f32[256,3,256]{2,0,1:T(8,128)}), f32[32,3,256]{2,0,1:T(8,128)}) %reduce-scatter.2.cloned.1.call-update) | async-done | bytes 98320 | tf_op jit(solution)/shard_map/while/body/eval_jaxpr/reduce_scatter | solution.py:65
  566.1 25.0 %all_gather.9 = bf16[3,256,256]{2,1,0:T(8,128)(2,1)S(1)} all-gather(bf16[3,32,256]{2,1,0:T(8,128)(2,1)S(1)} %get-tuple-element.321), channel_id=1, replica_groups=mesh['block'=4,'tok'=8] {'tok'}, dimensions={1}, use_global_device_ids=true | all-gather | bytes 442368 | tf_op jit(solution)/shard_map/while/body/eval_jaxpr/all_gather | solution.py:43
  601.4 68.2 %reduce-scatter.2.cloned.1.call-done = f32[32,3,256]{2,0,1:T(8,128)} async-done(((f32[256,3,256]{2,0,1:T(8,128)}), f32[32,3,256]{2,0,1:T(8,128)}) %reduce-scatter.2.cloned.1.call-update) | async-done | bytes 98320 | tf_op jit(solution)/shard_map/while/body/eval_jaxpr/reduce_scatter | solution.py:65
  677.5 25.0 %all_gather.9 = bf16[3,256,256]{2,1,0:T(8,128)(2,1)S(1)} all-gather(bf16[3,32,256]{2,1,0:T(8,128)(2,1)S(1)} %get-tuple-element.321), channel_id=1, replica_groups=mesh['block'=4,'tok'=8] {'tok'}, dimensions={1}, use_global_device_ids=true | all-gather | bytes 442368 | tf_op jit(solution)/shard_map/while/body/eval_jaxpr/all_gather | solution.py:43
  712.7 68.2 %reduce-scatter.2.cloned.1.call-done = f32[32,3,256]{2,0,1:T(8,128)} async-done(((f32[256,3,256]{2,0,1:T(8,128)}), f32[32,3,256]{2,0,1:T(8,128)}) %reduce-scatter.2.cloned.1.call-update) | async-done | bytes 98320 | tf_op jit(solution)/shard_map/while/body/eval_jaxpr/reduce_scatter | solution.py:65
  788.8 25.0 %all_gather.9 = bf16[3,256,256]{2,1,0:T(8,128)(2,1)S(1)} all-gather(bf16[3,32,256]{2,1,0:T(8,128)(2,1)S(1)} %get-tuple-element.321), channel_id=1, replica_groups=mesh['block'=4,'tok'=8] {'tok'}, dimensions={1}, use_global_device_ids=true | all-gather | bytes 442368 | tf_op jit(solution)/shard_map/while/body/eval_jaxpr/all_gather | solution.py:43
  824.1 68.2 %reduce-scatter.2.cloned.1.call-done = f32[32,3,256]{2,0,1:T(8,128)} async-done(((f32[256,3,256]{2,0,1:T(8,128)}), f32[32,3,256]{2,0,1:T(8,128)}) %reduce-scatter.2.cloned.1.call-update) | async-done | bytes 98320 | tf_op jit(solution)/shard_map/while/body/eval_jaxpr/reduce_scatter | solution.py:65
  900.2 25.0 %all_gather.9 = bf16[3,256,256]{2,1,0:T(8,128)(2,1)S(1)} all-gather(bf16[3,32,256]{2,1,0:T(8,128)(2,1)S(1)} %get-tuple-element.321), channel_id=1, replica_groups=mesh['block'=4,'tok'=8] {'tok'}, dimensions={1}, use_global_device_ids=true | all-gather | bytes 442368 | tf_op jit(solution)/shard_map/while/body/eval_jaxpr/all_gather | solution.py:43
  935.5 68.0 %reduce-scatter.2.cloned.1.call-done = f32[32,3,256]{2,0,1:T(8,128)} async-done(((f32[256,3,256]{2,0,1:T(8,128)}), f32[32,3,256]{2,0,1:T(8,128)}) %reduce-scatter.2.cloned.1.call-update) | async-done | bytes 98320 | tf_op jit(solution)/shard_map/while/body/eval_jaxpr/reduce_scatter | solution.py:65
  1011.5 25.0 %all_gather.9 = bf16[3,256,256]{2,1,0:T(8,128)(2,1)S(1)} all-gather(bf16[3,32,256]{2,1,0:T(8,128)(2,1)S(1)} %get-tuple-element.321), channel_id=1, replica_groups=mesh['block'=4,'tok'=8] {'tok'}, dimensions={1}, use_global_device_ids=true | all-gather | bytes 442368 | tf_op jit(solution)/shard_map/while/body/eval_jaxpr/all_gather | solution.py:43
  1046.8 68.1 %reduce-scatter.2.cloned.1.call-done = f32[32,3,256]{2,0,1:T(8,128)} async-done(((f32[256,3,256]{2,0,1:T(8,128)}), f32[32,3,256]{2,0,1:T(8,128)}) %reduce-scatter.2.cloned.1.call-update) | async-done | bytes 98320 | tf_op jit(solution)/shard_map/while/body/eval_jaxpr/reduce_scatter | solution.py:65
  1158.1 68.1 %reduce-scatter.2.cloned.1.call-done = f32[32,3,256]{2,0,1:T(8,128)} async-done(((f32[256,3,256]{2,0,1:T(8,128)}), f32[32,3,256]{2,0,1:T(8,128)}) %reduce-scatter.2.cloned.1.call-update) | async-done | bytes 98320 | tf_op jit(solution)/shard_map/while/body/eval_jaxpr/reduce_scatter | solution.py:65
  1269.4 68.2 %reduce-scatter.2.cloned.1.call-done = f32[32,3,256]{2,0,1:T(8,128)} async-done(((f32[256,3,256]{2,0,1:T(8,128)}), f32[32,3,256]{2,0,1:T(8,128)}) %reduce-scatter.2.cloned.1.call-update) | async-done | bytes 98320 | tf_op jit(solution)/shard_map/while/body/eval_jaxpr/reduce_scatter | solution.py:65
  1380.8 68.2 %reduce-scatter.2.cloned.1.call-done = f32[32,3,256]{2,0,1:T(8,128)} async-done(((f32[256,3,256]{2,0,1:T(8,128)}), f32[32,3,256]{2,0,1:T(8,128)}) %reduce-scatter.2.cloned.1.call-update) | async-done | bytes 98320 | tf_op jit(solution)/shard_map/while/body/eval_jaxpr/reduce_scatter | solution.py:65
  (242 shorter events, 312.9 us)
Async XLA Ops:
  8.7 104.0 %reduce-scatter.2.cloned.1.call-start = ((), (), s32[]{:S(2)}) async-start(), calls=%async_computation.1 | async-start | bytes 884736 | tf_op jit(solution)/shard_map/while/body/eval_jaxpr/reduce_scatter | solution.py:65
  114.7 5.1 collective-permute-start
  119.8 104.4 %reduce-scatter.2.cloned.1.call-start = ((), (), s32[]{:S(2)}) async-start(), calls=%async_computation.1 | async-start | bytes 884736 | tf_op jit(solution)/shard_map/while/body/eval_jaxpr/reduce_scatter | solution.py:65
  226.2 5.0 collective-permute-start
  231.2 104.3 %reduce-scatter.2.cloned.1.call-start = ((), (), s32[]{:S(2)}) async-start(), calls=%async_computation.1 | async-start | bytes 884736 | tf_op jit(solution)/shard_map/while/body/eval_jaxpr/reduce_scatter | solution.py:65
  337.4 5.0 collective-permute-start
  342.5 104.3 %reduce-scatter.2.cloned.1.call-start = ((), (), s32[]{:S(2)}) async-start(), calls=%async_computation.1 | async-start | bytes 884736 | tf_op jit(solution)/shard_map/while/body/eval_jaxpr/reduce_scatter | solution.py:65
  448.8 5.0 collective-permute-start
  453.8 104.3 %reduce-scatter.2.cloned.1.call-start = ((), (), s32[]{:S(2)}) async-start(), calls=%async_computation.1 | async-start | bytes 884736 | tf_op jit(solution)/shard_map/while/body/eval_jaxpr/reduce_scatter | solution.py:65
  560.1 5.0 collective-permute-start
  565.2 104.3 %reduce-scatter.2.cloned.1.call-start = ((), (), s32[]{:S(2)}) async-start(), calls=%async_computation.1 | async-start | bytes 884736 | tf_op jit(solution)/shard_map/while/body/eval_jaxpr/reduce_scatter | solution.py:65
  676.5 104.3 %reduce-scatter.2.cloned.1.call-start = ((), (), s32[]{:S(2)}) async-start(), calls=%async_computation.1 | async-start | bytes 884736 | tf_op jit(solution)/shard_map/while/body/eval_jaxpr/reduce_scatter | solution.py:65
  782.9 5.0 collective-permute-start
  787.9 104.3 %reduce-scatter.2.cloned.1.call-start = ((), (), s32[]{:S(2)}) async-start(), calls=%async_computation.1 | async-start | bytes 884736 | tf_op jit(solution)/shard_map/while/body/eval_jaxpr/reduce_scatter | solution.py:65
  894.3 5.0 collective-permute-start
  899.3 104.2 %reduce-scatter.2.cloned.1.call-start = ((), (), s32[]{:S(2)}) async-start(), calls=%async_computation.1 | async-start | bytes 884736 | tf_op jit(solution)/shard_map/while/body/eval_jaxpr/reduce_scatter | solution.py:65
  1005.5 5.0 collective-permute-start
  1010.6 104.3 %reduce-scatter.2.cloned.1.call-start = ((), (), s32[]{:S(2)}) async-start(), calls=%async_computation.1 | async-start | bytes 884736 | tf_op jit(solution)/shard_map/while/body/eval_jaxpr/reduce_scatter | solution.py:65
  1121.9 104.3 %reduce-scatter.2.cloned.1.call-start = ((), (), s32[]{:S(2)}) async-start(), calls=%async_computation.1 | async-start | bytes 884736 | tf_op jit(solution)/shard_map/while/body/eval_jaxpr/reduce_scatter | solution.py:65
  1228.2 5.0 collective-permute-start
  1233.3 104.3 %reduce-scatter.2.cloned.1.call-start = ((), (), s32[]{:S(2)}) async-start(), calls=%async_computation.1 | async-start | bytes 884736 | tf_op jit(solution)/shard_map/while/body/eval_jaxpr/reduce_scatter | solution.py:65
  1339.6 5.0 collective-permute-start
  1344.6 104.4 %reduce-scatter.2.cloned.1.call-start = ((), (), s32[]{:S(2)}) async-start(), calls=%async_computation.1 | async-start | bytes 884736 | tf_op jit(solution)/shard_map/while/body/eval_jaxpr/reduce_scatter | solution.py:65
  1451.0 5.0 collective-permute-start
  (3 other events, 11.0 us)
Sparse Core Ops, SparseCore 0:
  44.2 68.4 reduce-scatter.1
  154.9 69.2 reduce-scatter.1
  266.3 69.0 reduce-scatter.1
  377.6 69.1 reduce-scatter.1
  488.9 69.1 reduce-scatter.1
  600.3 69.1 reduce-scatter.1
  711.7 69.1 reduce-scatter.1
  823.0 69.1 reduce-scatter.1
  934.4 69.0 reduce-scatter.1
  1045.7 69.1 reduce-scatter.1
  1157.0 69.1 reduce-scatter.1
  1268.4 69.1 reduce-scatter.1
  1379.8 69.1 reduce-scatter.1
where the time goes:
time: 1470 us; the launch traced here: 1460 us
  waiting for transfers between devices  906 us (62%)
  blocking collectives  326 us (22%)
  matrix products  138 us (9%)
  other arithmetic  59.3 us (4%)
  starting transfers between devices  16.8 us (1%)
    reduce_scatter x13, waiting for transfers between devices, tick(): lax.psum_scatter(jnp.stack([across(d_a, keys), across(d_b, keys), across(...  885 us
    all_gather x13, blocking collectives, tick(): lax.all_gather(current.astype(jnp.bfloat16), 'tok', axis=1, tiled=True)  326 us
    dot_general x52, matrix products, against(): lax.dot_general(left, right, (((1,), (1,)), ((), ())), preferred_element_...  60.7 us
    dot_general x39, matrix products, across(): lax.dot_general(left, right, (((0,), (0,)), ((), ())), preferred_element_...  49.7 us
  transfers between devices with their start and end apart: 26, of which 26 were waited for; matrix products, arithmetic and copies ran while one was open for 3% of the time, Pallas kernels for 0%

commit v1 on v0

v1 whole, which is shorter than its diff:
```python
import functools
import math

import jax
import jax.numpy as jnp
from jax import lax
from jax.experimental import pallas as pl
from jax.experimental.pallas import tpu as pltpu
from jax.sharding import PartitionSpec as P

MESH = pl.DeviceIdType.MESH
PAIR = 2


def nt(left, right):
    return lax.dot_general(
        left, right, (((1,), (1,)), ((), ())), preferred_element_type=jnp.float32
    )


def nn(left, right):
    return lax.dot_general(
        left, right, (((1,), (0,)), ((), ())), preferred_element_type=jnp.float32
    )


def sigmoid(x):
    return 0.5 * jnp.tanh(0.5 * x) + 0.5


def kernel(
    heads, blocks, outer,
    q_ref, k_ref, g_ref, init_ref,
    out_ref, states_ref,
    wfull, iw, sw, wn, gf, gsum, sy, gy, sz, gz,
    wi_send, wz_send, wz_recv, wy_send, wy_recv, wn_send, wn_recv,
    gy_send, gy_recv, gz_send, gz_recv,
):
    b = lax.axis_index("block")
    t = lax.axis_index("tok")
    z, y = t // PAIR, t % PAIR
    rows = init_ref.shape[2]
    half = outer * rows
    mine = pl.ds(pl.multiple_of(y * half + z * rows, rows), rows)
    my_half = pl.ds(pl.multiple_of(y * half, half), half)
    its_half = pl.ds(pl.multiple_of((1 - y) * half, half), half)
    last = blocks - 1
    peer = (b, z * PAIR + (1 - y))

    def zid(d):
        return lax.rem(z + d, outer)

    def copy(src, dst, send, recv, dev):
        return pltpu.make_async_remote_copy(
            src_ref=src, dst_ref=dst, send_sem=send, recv_sem=recv,
            device_id=dev, device_id_type=MESH,
        )

    def init_copy(h, d):
        return copy(iw.at[h], wfull.at[h, :, mine, :], wi_send.at[h, d], wz_recv.at[h, z],
                    (b, zid(d) * PAIR + y))

    def next_copy(h, d):
        return copy(sw.at[h], wfull.at[h, :, mine, :], wz_send.at[h, d], wz_recv.at[h, z],
                    (lax.rem(b + 1, blocks), zid(d) * PAIR + y))

    def wz_arrival(h, d):
        start = pl.multiple_of(y * half + zid(d) * rows, rows)
        return copy(sw.at[h], wfull.at[h, :, pl.ds(start, rows), :], wz_send.at[h, d],
                    wz_recv.at[h, zid(d)], peer)

    def pass_copy(h):
        return copy(states_ref.at[h], wn.at[h], wn_send.at[h], wn_recv.at[h],
                    (lax.rem(b + 1, blocks), t))

    def fwd_copy(h):
        view = wfull.at[h, :, my_half, :]
        return copy(view, view, wy_send.at[h], wy_recv.at[h], peer)

    def fwd_arrival(h):
        view = wfull.at[h, :, its_half, :]
        return copy(view, view, wy_send.at[h], wy_recv.at[h], peer)

    def gy_copy(h, m):
        return copy(sy.at[h, m], gy.at[h, m], gy_send.at[h, m], gy_recv.at[h, m], peer)

    def gz_copy(h, d):
        part = pl.ds(pl.multiple_of(zid(d) * rows, rows), rows)
        return copy(sz.at[h, :, part, :], gz.at[h, z], gz_send.at[h, d], gz_recv.at[h, z],
                    (b, zid(d) * PAIR + y))

    def gz_arrival(h, d):
        return copy(sz.at[h, :, pl.ds(0, rows), :], gz.at[h, zid(d)], gz_send.at[h, d],
                    gz_recv.at[h, zid(d)], peer)

    barrier = pltpu.get_barrier_semaphore()

    def greet(dev):
        pl.semaphore_signal(barrier, inc=1, device_id=dev, device_id_type=MESH)

    greet(peer)
    for d in range(1, outer):
        greet((b, zid(d) * PAIR + y))

    for d in range(outer):
        greet((lax.rem(b + 1, blocks), zid(d) * PAIR + y))
        greet((lax.rem(b + last, blocks), zid(d) * PAIR + y))
    pl.semaphore_wait(barrier, 3 * outer)

    def start_init(h):
        iw[h] = init_ref[h].astype(jnp.bfloat16)
        wfull[h, :, mine, :] = iw[h]
        for d in range(1, outer):
            init_copy(h, d).start()

    def forward_weights(h):
        for d in range(1, outer):
            wz_arrival(h, d).wait_recv()

        @pl.when(b > 0)
        def _():
            wz_arrival(h, 0).wait_recv()

        fwd_copy(h).start()

    @pl.when(b == 0)
    def _():
        start_init(0)
        start_init(1)

    forward_weights(0)

    def one_head(h, _):
        fwd_arrival(h).wait_recv()
        wa, wb, wc = wfull[h, 0], wfull[h, 1], wfull[h, 2]
        keys, g = k_ref[h], g_ref[h]

        def emit(m, grad):
            gf[m] = grad
            sy[h, m] = gf[m, its_half, :].astype(jnp.bfloat16)
            gy_copy(h, m).start()

        a = nt(wa, keys)
        bb = nt(wb, keys)
        sig = sigmoid(a)
        s = a * sig
        emit(2, nn((s * bb).astype(jnp.bfloat16), g))
        dhid = nt(wc, g)
        emit(1, nn((dhid * s).astype(jnp.bfloat16), keys))
        dsil = sig * (1.0 + a * (1.0 - sig))
        emit(0, nn((dhid * bb * dsil).astype(jnp.bfloat16), keys))

        @pl.when((b == 0) & (h + 2 < heads))
        def _():
            start_init(h + 2)

        @pl.when((b == 0) & (h + 1 < heads))
        def _():
            forward_weights(h + 1)

        for m in (2, 1, 0):
            gy_copy(h, m).wait_recv()
            total = gf[m, my_half, :] + gy[h, m].astype(jnp.float32)
            gsum[m] = total
            sz[h, m] = total.astype(jnp.bfloat16)
        for d in range(1, outer):
            gz_copy(h, d).start()

        quer = q_ref[h]
        qa = nt(quer, wa)
        hid_q = (qa * sigmoid(qa) * nt(quer, wb)).astype(jnp.bfloat16)
        out_ref[h] = nn(hid_q, wc).astype(jnp.bfloat16)

        @pl.when(b == 0)
        def _():
            wn[h] = init_ref[h]

        @pl.when(b > 0)
        def _():
            pass_copy(h).wait_recv()

        current = wn[h]
        grads = gsum[:, pl.ds(pl.multiple_of(z * rows, rows), rows), :]
        for d in range(1, outer):
            gz_arrival(h, d).wait_recv()
            grads = grads + gz[h, zid(d)].astype(jnp.float32)
        upd = current - grads
        ratio = jnp.sqrt(
            (jnp.mean(current * current, axis=-1, keepdims=True) + 1e-06)
            / (jnp.mean(upd * upd, axis=-1, keepdims=True) + 1e-06)
        )
        new_w = upd * ratio
        states_ref[h] = new_w
        sw[h] = new_w.astype(jnp.bfloat16)

        @pl.when(b < last)
        def _():
            for d in range(outer):
                next_copy(h, d).start()
            pass_copy(h).start()

        @pl.when((b > 0) & (h + 1 < heads))
        def _():
            forward_weights(h + 1)

        return 0

    lax.fori_loop(0, heads, one_head, 0)

    def drain(h, _):
        @pl.when(b == 0)
        def _():
            for d in range(1, outer):
                init_copy(h, d).wait_send()

        @pl.when(b < last)
        def _():
            for d in range(outer):
                next_copy(h, d).wait_send()
            pass_copy(h).wait_send()

        fwd_copy(h).wait_send()
        for m in range(3):
            gy_copy(h, m).wait_send()
        for d in range(1, outer):
            gz_copy(h, d).wait_send()
        return 0

    lax.fori_loop(0, heads, drain, 0)


def on_device(query, key, value, rates, init_weights):
    tokens, heads, dim = query.shape
    blocks, tok = lax.axis_size("block"), lax.axis_size("tok")
    outer = tok // PAIR
    rows, hid = init_weights.shape[2], init_weights.shape[2] * tok
    half = hid // PAIR
    factor = rates * (1.0 / math.sqrt(tokens * tok))
    g = (-(factor[:, :, None] * jnp.transpose(value, (1, 0, 2)).astype(jnp.float32))).astype(jnp.bfloat16)
    q = jnp.transpose(query, (1, 0, 2))
    k = jnp.transpose(key, (1, 0, 2))
    bf16, f32 = jnp.bfloat16, jnp.float32
    dma = pltpu.SemaphoreType.DMA
    vmem = pl.BlockSpec(memory_space=pltpu.VMEM)
    out, states = pl.pallas_call(
        functools.partial(kernel, heads, blocks, outer),
        out_shape=(
            jax.ShapeDtypeStruct((heads, tokens, dim), bf16),
            jax.ShapeDtypeStruct(init_weights.shape, f32),
        ),
        in_specs=[vmem] * 4,
        out_specs=(vmem, vmem),
        scratch_shapes=[
            pltpu.VMEM((heads, 3, hid, dim), bf16),
            pltpu.VMEM((heads, 3, rows, dim), bf16),
            pltpu.VMEM((heads, 3, rows, dim), bf16),
            pltpu.VMEM((heads, 3, rows, dim), f32),
            pltpu.VMEM((3, hid, dim), f32),
            pltpu.VMEM((3, half, dim), f32),
            pltpu.VMEM((heads, 3, half, dim), bf16),
            pltpu.VMEM((heads, 3, half, dim), bf16),
            pltpu.VMEM((heads, 3, half, dim), bf16),
            pltpu.VMEM((heads, outer, 3, rows, dim), bf16),
            dma((heads, outer)), dma((heads, outer)), dma((heads, outer)),
            dma((heads,)), dma((heads,)), dma((heads,)), dma((heads,)),
            dma((heads, 3)), dma((heads, 3)),
            dma((heads, outer)), dma((heads, outer)),
        ],
        compiler_params=pltpu.CompilerParams(
            collective_id=0, has_side_effects=True, vmem_limit_bytes=48 * 1024 * 1024
        ),
        cost_estimate=pl.CostEstimate(
            flops=18 * heads * tokens * hid * dim,
            bytes_accessed=10 * heads * tokens * dim,
            transcendentals=2 * heads * tokens * hid,
        ),
    )(q, k, g, init_weights)
    return (jnp.transpose(out, (1, 0, 2)), states[None])


def solution(mesh):
    placed = (
        P(("block", "tok"), None, None),
        P(("block", "tok"), None, None),
        P(("block", "tok"), None, None),
        P(None, ("block", "tok")),
        P(None, None, "tok", None),
    )
    return jax.shard_map(
        on_device,
        mesh=mesh,
        in_specs=placed,
        out_specs=(P(("block", "tok"), None, None), P("block", None, None, "tok", None)),
        check_vma=False,
    )
```

time: 1470 us -> 239 us (0.16)
  waiting for transfers between devices: 906 us -> 0 us
  blocking collectives: 326 us -> 0 us
  Pallas kernels: 0 us -> 232 us
  matrix products: 138 us -> 0 us
  other arithmetic: 59.3 us -> 3.71 us
  starting transfers between devices: 16.8 us -> 0 us
    reduce_scatter x13 -> x0, waiting for transfers between devices: 885 us -> none  [tick(): lax.psum_scatter(jnp.stack([across(d_a, keys), across(d_b, keys), across(...]
    all_gather x13 -> x0, blocking collectives: 326 us -> none  [tick(): lax.all_gather(current.astype(jnp.bfloat16), 'tok', axis=1, tiled=True)]
    pallas_call x0 -> x1, Pallas kernels: none -> 232 us  [on_device(): pl.pallas_call(functools.partial(kernel, heads, blocks, outer), out_shape...]
    dot_general x104 -> x0, matrix products: 138 us -> none  [the longest x52 60.7 us: against(): lax.dot_general(left, right, (((1,), (1,)), ((), ())), preferred_element_...]
    ppermute x13 -> x0, waiting for transfers between devices: 21.2 us -> none  [passed_along(): lax.ppermute(value, axis, [(source, source + steps) for source in range(l...]
    ppermute x13 -> x0, starting transfers between devices: 16.8 us -> none  [passed_along(): lax.ppermute(value, axis, [(source, source + steps) for source in range(l...]
  transfers between devices with their start and end apart: 26 -> 0, of which waited for: 26 -> 0; matrix products, arithmetic and copies ran while one was open for 3% -> 0% of each run, Pallas kernels for 0% -> 0%
where the time goes in v1:
time: 239 us
  Pallas kernels  232 us (97%)
  other arithmetic  3.71 us (2%)
    pallas_call x1, Pallas kernels, on_device(): pl.pallas_call(functools.partial(kernel, heads, blocks, outer), out_shape...  232 us

profile of v1, /device:TPU:3, one launch (start us, length us, event | category | flops | bytes accessed | tf_op | source)
XLA Modules:
  0.0 238.7 jit_solution(17745547056781938445)
XLA Ops:
  0.6 0.7 broadcast_multiply_fusion
  1.4 0.0 copy-start
  1.4 0.0 copy-start.1
  1.4 3.0 %fusion.1.g_ref = bf16[10,384,256]{2,1,0:T(8,128)(2,1)} fusion(bf16[384,10,256]{2,0,1:T(8,128)(2,1)} %param.7, f32[10,384]{1,0:T(8,128)S(1)} %broadcast_multiply_fusion), kind=kLoop, calls=%fused_computation.2 | loop fusion | flops 3932160 | bytes 3947520 | tf_op jit(solution)/shard_map/convert_element_type | solution.py:239
  4.3 0.0 copy-done
  4.4 0.0 copy-done.1
  4.4 232.1 %shard_map.68 = (bf16[10,384,256]{2,1,0:T(8,128)(2,1)S(1)}, f32[10,3,32,256]{3,2,1,0:T(8,128)S(1)}) custom-call(bf16[10,384,256]{2,1,0:T(8,128)(2,1)S(1)} %bitcast.12, bf16[10,384,256]{2,1,0:T(8,128)(2,1)} %bitcast.13, bf16[10,384,256]{2,1,0:T(8,128)(2,1)} %fusion.1.g_ref, f32[10,3,32,256]{3,2,1,0:T(8,128)S(1)} %copy-done.1), custom_call_target="tpu_custom_call" | custom-call | flops 4529848320 | bytes 9830400 | tf_op jit(solution)/shard_map/pallas_call | solution.py:245
  236.5 1.3 copy.9
  237.8 0.9 copy.10
Async XLA Ops:
  1.4 3.0 %copy-start = (bf16[384,10,256]{2,0,1:T(8,128)(2,1)S(1)}, bf16[384,10,256]{2,0,1:T(8,128)(2,1)}, u32[]{:S(2)}) copy-start(bf16[384,10,256]{2,0,1:T(8,128)(2,1)} %param.5) | copy-start | bytes 5898244
  1.4 3.0 %copy-start.1 = (f32[10,3,32,256]{3,2,1,0:T(8,128)S(1)}, f32[10,3,32,256]{3,2,1,0:T(8,128)}, u32[]{:S(2)}) copy-start(f32[10,3,32,256]{3,2,1,0:T(8,128)} %init_ref.1) | copy-start | bytes 2949124

commit v2 on v1

--- a/solution.py
+++ b/solution.py
@@ -9,6 +9,9 @@
 from jax.sharding import PartitionSpec as P
 
 MESH = pl.DeviceIdType.MESH
+LEAD = 1
+DEPTH = 2
+AHEAD = 3
 PAIR = 2
 
 
@@ -125,19 +128,20 @@
 
     @pl.when(b == 0)
     def _():
-        start_init(0)
-        start_init(1)
-
-    forward_weights(0)
-
-    def one_head(h, _):
+        for h in range(min(AHEAD, heads)):
+            start_init(h)
+
+    for h in range(min(LEAD, heads)):
+        forward_weights(h)
+
+    def differentiate(h):
         fwd_arrival(h).wait_recv()
         wa, wb, wc = wfull[h, 0], wfull[h, 1], wfull[h, 2]
         keys, g = k_ref[h], g_ref[h]
 
         def emit(m, grad):
-            gf[m] = grad
-            sy[h, m] = gf[m, its_half, :].astype(jnp.bfloat16)
+            gf[h, m] = grad
+            sy[h, m] = gf[h, m, its_half, :].astype(jnp.bfloat16)
             gy_copy(h, m).start()
 
         a = nt(wa, keys)
@@ -150,27 +154,23 @@
         dsil = sig * (1.0 + a * (1.0 - sig))
         emit(0, nn((dhid * bb * dsil).astype(jnp.bfloat16), keys))
 
-        @pl.when((b == 0) & (h + 2 < heads))
-        def _():
-            start_init(h + 2)
-
-        @pl.when((b == 0) & (h + 1 < heads))
-        def _():
-            forward_weights(h + 1)
-
+    def combine(h):
         for m in (2, 1, 0):
             gy_copy(h, m).wait_recv()
-            total = gf[m, my_half, :] + gy[h, m].astype(jnp.float32)
-            gsum[m] = total
+            total = gf[h, m, my_half, :] + gy[h, m].astype(jnp.float32)
+            gsum[h, m] = total
             sz[h, m] = total.astype(jnp.bfloat16)
         for d in range(1, outer):
             gz_copy(h, d).start()
 
+    def answer(h):
+        wa, wb, wc = wfull[h, 0], wfull[h, 1], wfull[h, 2]
         quer = q_ref[h]
         qa = nt(quer, wa)
         hid_q = (qa * sigmoid(qa) * nt(quer, wb)).astype(jnp.bfloat16)
         out_ref[h] = nn(hid_q, wc).astype(jnp.bfloat16)
 
+    def update(h):
         @pl.when(b == 0)
         def _():
             wn[h] = init_ref[h]
@@ -180,7 +180,7 @@
             pass_copy(h).wait_recv()
 
         current = wn[h]
-        grads = gsum[:, pl.ds(pl.multiple_of(z * rows, rows), rows), :]
+        grads = gsum[h, :, pl.ds(pl.multiple_of(z * rows, rows), rows), :]
         for d in range(1, outer):
             gz_arrival(h, d).wait_recv()
             grads = grads + gz[h, zid(d)].astype(jnp.float32)
@@ -199,13 +199,25 @@
                 next_copy(h, d).start()
             pass_copy(h).start()
 
-        @pl.when((b > 0) & (h + 1 < heads))
-        def _():
-            forward_weights(h + 1)
-
+    def guarded(fn, h, cond=None):
+        ok = (h >= 0) & (h < heads)
+        if cond is not None:
+            ok = ok & cond
+
+        @pl.when(ok)
+        def _():
+            fn(h)
+
+    def step(i, _):
+        guarded(start_init, i + AHEAD, b == 0)
+        guarded(update, i - 2)
+        guarded(combine, i - 1)
+        guarded(differentiate, i + 0)
+        guarded(forward_weights, i + 1)
+        guarded(answer, i + 0)
         return 0
 
-    lax.fori_loop(0, heads, one_head, 0)
+    lax.fori_loop(0, heads + DEPTH, step, 0)
 
     def drain(h, _):
         @pl.when(b == 0)
@@ -255,8 +267,8 @@
             pltpu.VMEM((heads, 3, rows, dim), bf16),
             pltpu.VMEM((heads, 3, rows, dim), bf16),
             pltpu.VMEM((heads, 3, rows, dim), f32),
-            pltpu.VMEM((3, hid, dim), f32),
-            pltpu.VMEM((3, half, dim), f32),
+            pltpu.VMEM((heads, 3, hid, dim), f32),
+            pltpu.VMEM((heads, 3, half, dim), f32),
             pltpu.VMEM((heads, 3, half, dim), bf16),
             pltpu.VMEM((heads, 3, half, dim), bf16),
             pltpu.VMEM((heads, 3, half, dim), bf16),

time: 239 us -> 191 us (0.80)
  Pallas kernels: 232 us -> 183 us
    pallas_call x1, Pallas kernels: 232 us -> 183 us  [on_device(): pl.pallas_call(functools.partial(kernel, heads, blocks, outer), out_shape...]
where the time goes in v2:
time: 191 us; the launch traced here: 189 us
  Pallas kernels  183 us (96%)
  other arithmetic  3.71 us (2%)
  local copies, waits for them, and re-layouts  2.23 us (1%)
    pallas_call x1, Pallas kernels, on_device(): pl.pallas_call(functools.partial(kernel, heads, blocks, outer), out_shape...  183 us

profile of v2, /device:TPU:3, one launch (start us, length us, event | category | flops | bytes accessed | tf_op | source)
XLA Modules:
  0.0 189.2 jit_solution(5450748519823142446)
XLA Ops:
  0.6 0.7 broadcast_multiply_fusion
  1.4 0.0 copy-start
  1.4 0.0 copy-start.1
  1.4 3.0 %fusion.1.g_ref = bf16[10,384,256]{2,1,0:T(8,128)(2,1)} fusion(bf16[384,10,256]{2,0,1:T(8,128)(2,1)} %param.7, f32[10,384]{1,0:T(8,128)S(1)} %broadcast_multiply_fusion), kind=kLoop, calls=%fused_computation.2 | loop fusion | flops 3932160 | bytes 3947520 | tf_op jit(solution)/shard_map/convert_element_type | solution.py:251
  4.3 0.0 copy-done
  4.4 0.0 copy-done.1
  4.4 182.6 %shard_map.68 = (bf16[10,384,256]{2,1,0:T(8,128)(2,1)S(1)}, f32[10,3,32,256]{3,2,1,0:T(8,128)S(1)}) custom-call(bf16[10,384,256]{2,1,0:T(8,128)(2,1)S(1)} %bitcast.12, bf16[10,384,256]{2,1,0:T(8,128)(2,1)} %bitcast.13, bf16[10,384,256]{2,1,0:T(8,128)(2,1)} %fusion.1.g_ref, f32[10,3,32,256]{3,2,1,0:T(8,128)S(1)} %copy-done.1), custom_call_target="tpu_custom_call" | custom-call | flops 4529848320 | bytes 9830400 | tf_op jit(solution)/shard_map/pallas_call | solution.py:257
  187.0 1.3 copy.9
  188.2 0.9 copy.10
Async XLA Ops:
  1.4 3.0 %copy-start = (bf16[384,10,256]{2,0,1:T(8,128)(2,1)S(1)}, bf16[384,10,256]{2,0,1:T(8,128)(2,1)}, u32[]{:S(2)}) copy-start(bf16[384,10,256]{2,0,1:T(8,128)(2,1)} %param.5) | copy-start | bytes 5898244
  1.4 3.0 %copy-start.1 = (f32[10,3,32,256]{3,2,1,0:T(8,128)S(1)}, f32[10,3,32,256]{3,2,1,0:T(8,128)}, u32[]{:S(2)}) copy-start(f32[10,3,32,256]{3,2,1,0:T(8,128)} %init_ref.1) | copy-start | bytes 2949124

commit v3 on v1

v3 whole, which is shorter than its diff:
```python
import functools
import math

import jax
import jax.numpy as jnp
from jax import lax
from jax.experimental import pallas as pl
from jax.experimental.pallas import tpu as pltpu
from jax.sharding import PartitionSpec as P

MESH = pl.DeviceIdType.MESH
AHEAD = 1
PAIR = 2


def nt(left, right):
    return lax.dot_general(
        left, right, (((1,), (1,)), ((), ())), preferred_element_type=jnp.float32
    )


def nn(left, right):
    return lax.dot_general(
        left, right, (((1,), (0,)), ((), ())), preferred_element_type=jnp.float32
    )


def sigmoid(x):
    return 0.5 * jnp.tanh(0.5 * x) + 0.5


def kernel(
    heads, blocks, outer,
    q_ref, k_ref, g_ref, init_ref,
    out_ref, states_ref,
    wfull, wq, kp, gp, wn, nw, sw, iw, ip, sp, gf, sz, gz,
    kp_send, kp_recv, gp_send, gp_recv, ip_send, ip_recv, sp_send, sp_recv,
    wn_send, wn_recv, wq_send, wq_recv, wi_send, wz_send, wz_recv, gz_send, gz_recv,
):
    b = lax.axis_index("block")
    t = lax.axis_index("tok")
    z, y = t // PAIR, t % PAIR
    n = heads // PAIR
    rows = init_ref.shape[2]
    quarter = PAIR * rows
    my_rows = pl.ds(pl.multiple_of(y * rows, rows), rows)
    its_rows = pl.ds(pl.multiple_of((1 - y) * rows, rows), rows)
    last = blocks - 1
    late = b >= blocks // 2
    peer = (b, z * PAIR + (1 - y))
    following = lax.rem(b + 1, blocks)

    def zid(d):
        return lax.rem(z + d, outer)

    def part(d):
        return pl.ds(pl.multiple_of(zid(d) * quarter, quarter), quarter)

    def own(j):
        return y * n + j

    def other(j):
        return (1 - y) * n + j

    def copy(src, dst, send, recv, dev):
        return pltpu.make_async_remote_copy(
            src_ref=src, dst_ref=dst, send_sem=send, recv_sem=recv,
            device_id=dev, device_id_type=MESH,
        )

    def key_copy(j):
        return copy(k_ref.at[other(j)], kp.at[j], kp_send.at[j], kp_recv.at[j], peer)

    def g_copy(j):
        return copy(g_ref.at[other(j)], gp.at[j], gp_send.at[j], gp_recv.at[j], peer)

    def ip_copy(j):
        return copy(init_ref.at[other(j)], ip.at[j], ip_send.at[j], ip_recv.at[j], peer)

    def sp_copy(j):
        return copy(nw.at[j, :, its_rows, :], sp.at[j], sp_send.at[j], sp_recv.at[j], peer)

    def wq_copy(j):
        return copy(wfull.at[j], wq.at[j], wq_send.at[j], wq_recv.at[j], peer)

    def init_copy(j, d):
        return copy(iw.at[j], wfull.at[j, :, part(0), :], wi_send.at[j, d], wz_recv.at[j, z],
                    (b, zid(d) * PAIR + y))

    def next_copy(j, d):
        return copy(sw.at[j], wfull.at[j, :, part(0), :], wz_send.at[j, d], wz_recv.at[j, z],
                    (following, zid(d) * PAIR + y))

    def wz_arrival(j, d):
        return copy(sw.at[j], wfull.at[j, :, part(d), :], wz_send.at[j, d],
                    wz_recv.at[j, zid(d)], peer)

    def pass_copy(j):
        return copy(nw.at[j], wn.at[j], wn_send.at[j], wn_recv.at[j], (following, t))

    def gz_copy(j, d):
        return copy(sz.at[j, :, part(d), :], gz.at[j, z], gz_send.at[j, d], gz_recv.at[j, z],
                    (b, zid(d) * PAIR + y))

    def gz_arrival(j, d):
        return copy(sz.at[j, :, part(d), :], gz.at[j, zid(d)], gz_send.at[j, d],
                    gz_recv.at[j, zid(d)], peer)

    barrier = pltpu.get_barrier_semaphore()

    def greet(dev):
        pl.semaphore_signal(barrier, inc=1, device_id=dev, device_id_type=MESH)

    greet(peer)
    for d in range(1, outer):
        greet((b, zid(d) * PAIR + y))
    for d in range(outer):
        greet((following, zid(d) * PAIR + y))
        greet((lax.rem(b + last, blocks), zid(d) * PAIR + y))
    pl.semaphore_wait(barrier, 3 * outer)

    def start_tokens(j):
        @pl.when(b == 0)
        def _():
            ip_copy(j).start()

        key_copy(j).start()
        g_copy(j).start()

    def start_init(j):
        ip_copy(j).wait_recv()
        wn[j, :, my_rows, :] = init_ref[own(j)]
        wn[j, :, its_rows, :] = ip[j]
        iw[j] = wn[j].astype(jnp.bfloat16)
        wfull[j, :, part(0), :] = iw[j]
        for d in range(1, outer):
            init_copy(j, d).start()

    for j in range(min(AHEAD, n)):
        start_tokens(j)

    @pl.when(late)
    def _():
        for j in range(min(AHEAD, n), n):
            start_tokens(j)

    @pl.when(b == 0)
    def _():
        for j in range(min(AHEAD, n)):
            start_init(j)

    def differentiate(j):
        for d in range(1, outer):
            wz_arrival(j, d).wait_recv()

        @pl.when(b > 0)
        def _():
            wz_arrival(j, 0).wait_recv()

        key_copy(j).wait_recv()
        g_copy(j).wait_recv()
        wa, wb, wc = wfull[j, 0], wfull[j, 1], wfull[j, 2]

        def terms(keys, g):
            a = nt(wa, keys)
            bb = nt(wb, keys)
            sig = sigmoid(a)
            s = a * sig
            hid = (s * bb).astype(jnp.bfloat16)
            dhid = nt(wc, g)
            db = (dhid * s).astype(jnp.bfloat16)
            da = (dhid * bb * (sig * (1.0 + a * (1.0 - sig)))).astype(jnp.bfloat16)
            return nn(da, keys), nn(db, keys), nn(hid, g)

        for m, grad in enumerate(terms(k_ref[own(j)], g_ref[own(j)])):
            gf[j, m] = grad
        for m, grad in enumerate(terms(kp[j], gp[j])):
            total = gf[j, m] + grad
            gf[j, m] = total
            sz[j, m] = total.astype(jnp.bfloat16)
        for d in range(1, outer):
            gz_copy(j, d).start()

    def lend(j):
        wq_copy(j).start()

    def respond(h, weights, j):
        quer = q_ref[h]
        qa = nt(quer, weights[j, 0])
        hid_q = (qa * sigmoid(qa) * nt(quer, weights[j, 1])).astype(jnp.bfloat16)
        out_ref[h] = nn(hid_q, weights[j, 2]).astype(jnp.bfloat16)

    def answer(j):
        respond(own(j), wfull, j)

    def answer_other(j):
        wq_copy(j).wait_recv()
        respond(other(j), wq, j)

    def update(j):
        @pl.when(b > 0)
        def _():
            pass_copy(j).wait_recv()

        current = wn[j]
        grads = gf[j, :, part(0), :]
        for d in range(1, outer):
            gz_arrival(j, d).wait_recv()
            grads = grads + gz[j, zid(d)].astype(jnp.float32)
        upd = current - grads
        ratio = jnp.sqrt(
            (jnp.mean(current * current, axis=-1, keepdims=True) + 1e-06)
            / (jnp.mean(upd * upd, axis=-1, keepdims=True) + 1e-06)
        )
        new_w = upd * ratio
        nw[j] = new_w
        sw[j] = new_w.astype(jnp.bfloat16)

        @pl.when(b < last)
        def _():
            for d in range(outer):
                next_copy(j, d).start()
            pass_copy(j).start()

        sp_copy(j).start()
        states_ref[own(j)] = nw[j, :, my_rows, :]

    def guarded(fn, j, cond=None):
        ok = (j >= 0) & (j < n)
        if cond is not None:
            ok = ok & cond

        @pl.when(ok)
        def _():
            fn(j)

    def step(i, _):
        guarded(differentiate, i)
        guarded(start_tokens, i + AHEAD, jnp.logical_not(late))
        guarded(start_init, i + AHEAD, b == 0)
        guarded(lend, i, late)
        guarded(answer, i)
        guarded(answer_other, i - 1, late)
        guarded(update, i)
        return 0

    lax.fori_loop(0, n + 1, step, 0)

    def finish(j, _):
        lend(j)
        return 0

    def finish_other(j, _):
        answer_other(j)
        return 0

    @pl.when(jnp.logical_not(late))
    def _():
        lax.fori_loop(0, n, finish, 0)
        lax.fori_loop(0, n, finish_other, 0)

    def drain(j, _):
        sp_copy(j).wait_recv()
        states_ref[other(j)] = sp[j]

        @pl.when(b == 0)
        def _():
            ip_copy(j).wait_send()
            for d in range(1, outer):
                init_copy(j, d).wait_send()

        @pl.when(b < last)
        def _():
            for d in range(outer):
                next_copy(j, d).wait_send()
            pass_copy(j).wait_send()

        key_copy(j).wait_send()
        g_copy(j).wait_send()
        sp_copy(j).wait_send()
        wq_copy(j).wait_send()
        for d in range(1, outer):
            gz_copy(j, d).wait_send()
        return 0

    lax.fori_loop(0, n, drain, 0)


def on_device(query, key, value, rates, init_weights):
    tokens, heads, dim = query.shape
    blocks, tok = lax.axis_size("block"), lax.axis_size("tok")
    outer = tok // PAIR
    rows, hid = init_weights.shape[2], init_weights.shape[2] * tok
    quarter, n = PAIR * rows, heads // PAIR
    factor = rates * (1.0 / math.sqrt(tokens * tok))
    g = (-(factor[:, :, None] * jnp.transpose(value, (1, 0, 2)).astype(jnp.float32))).astype(jnp.bfloat16)
    q = jnp.transpose(query, (1, 0, 2))
    k = jnp.transpose(key, (1, 0, 2))
    bf16, f32 = jnp.bfloat16, jnp.float32
    dma = pltpu.SemaphoreType.DMA
    vmem = pl.BlockSpec(memory_space=pltpu.VMEM)
    out, states = pl.pallas_call(
        functools.partial(kernel, heads, blocks, outer),
        out_shape=(
            jax.ShapeDtypeStruct((heads, tokens, dim), bf16),
            jax.ShapeDtypeStruct(init_weights.shape, f32),
        ),
        in_specs=[vmem] * 4,
        out_specs=(vmem, vmem),
        scratch_shapes=[
            pltpu.VMEM((n, 3, hid, dim), bf16),
            pltpu.VMEM((n, 3, hid, dim), bf16),
            pltpu.VMEM((n, tokens, dim), bf16),
            pltpu.VMEM((n, tokens, dim), bf16),
            pltpu.VMEM((n, 3, quarter, dim), f32),
            pltpu.VMEM((n, 3, quarter, dim), f32),
            pltpu.VMEM((n, 3, quarter, dim), bf16),
            pltpu.VMEM((n, 3, quarter, dim), bf16),
            pltpu.VMEM((n, 3, rows, dim), f32),
            pltpu.VMEM((n, 3, rows, dim), f32),
            pltpu.VMEM((n, 3, hid, dim), f32),
            pltpu.VMEM((n, 3, hid, dim), bf16),
            pltpu.VMEM((n, outer, 3, quarter, dim), bf16),
        ] + [dma((n,))] * 12 + [dma((n, outer))] * 5,
        compiler_params=pltpu.CompilerParams(
            collective_id=0, has_side_effects=True, vmem_limit_bytes=48 * 1024 * 1024
        ),
        cost_estimate=pl.CostEstimate(
            flops=18 * heads * tokens * hid * dim,
            bytes_accessed=10 * heads * tokens * dim,
            transcendentals=2 * heads * tokens * hid,
        ),
    )(q, k, g, init_weights)
    return (jnp.transpose(out, (1, 0, 2)), states[None])


def solution(mesh):
    placed = (
        P(("block", "tok"), None, None),
        P(("block", "tok"), None, None),
        P(("block", "tok"), None, None),
        P(None, ("block", "tok")),
        P(None, None, "tok", None),
    )
    return jax.shard_map(
        on_device,
        mesh=mesh,
        in_specs=placed,
        out_specs=(P(("block", "tok"), None, None), P("block", None, None, "tok", None)),
        check_vma=False,
    )
```

time: 239 us -> 168 us (0.70)
  Pallas kernels: 232 us -> 161 us
    pallas_call x1, Pallas kernels: 232 us -> 161 us  [on_device(): pl.pallas_call(functools.partial(kernel, heads, blocks, outer), out_shape...]
where the time goes in v3:
time: 168 us
  Pallas kernels  161 us (96%)
  other arithmetic  3.71 us (2%)
  local copies, waits for them, and re-layouts  2.23 us (1%)
    pallas_call x1, Pallas kernels, on_device(): pl.pallas_call(functools.partial(kernel, heads, blocks, outer), out_shape...  161 us

profile of v3, /device:TPU:3, one launch (start us, length us, event | category | flops | bytes accessed | tf_op | source)
XLA Modules:
  0.0 167.6 jit_solution(3749052772350243286)
XLA Ops:
  0.6 0.7 broadcast_multiply_fusion
  1.4 0.0 copy-start
  1.4 0.0 copy-start.1
  1.4 3.0 %fusion.1.g_ref = bf16[10,384,256]{2,1,0:T(8,128)(2,1)} fusion(bf16[384,10,256]{2,0,1:T(8,128)(2,1)} %param.7, f32[10,384]{1,0:T(8,128)S(1)} %broadcast_multiply_fusion), kind=kLoop, calls=%fused_computation.2 | loop fusion | flops 3932160 | bytes 3947520 | tf_op jit(solution)/shard_map/convert_element_type | solution.py:296
  4.3 0.0 copy-done
  4.4 0.0 copy-done.1
  4.4 161.0 %shard_map.68 = (bf16[10,384,256]{2,1,0:T(8,128)(2,1)S(1)}, f32[10,3,32,256]{3,2,1,0:T(8,128)S(1)}) custom-call(bf16[10,384,256]{2,1,0:T(8,128)(2,1)S(1)} %bitcast.12, bf16[10,384,256]{2,1,0:T(8,128)(2,1)} %bitcast.13, bf16[10,384,256]{2,1,0:T(8,128)(2,1)} %fusion.1.g_ref, f32[10,3,32,256]{3,2,1,0:T(8,128)S(1)} %copy-done.1), custom_call_target="tpu_custom_call" | custom-call | flops 4529848320 | bytes 9830400 | tf_op jit(solution)/shard_map/pallas_call | solution.py:302
  165.4 1.3 copy.9
  166.6 0.9 copy.10
Async XLA Ops:
  1.4 3.0 %copy-start = (bf16[384,10,256]{2,0,1:T(8,128)(2,1)S(1)}, bf16[384,10,256]{2,0,1:T(8,128)(2,1)}, u32[]{:S(2)}) copy-start(bf16[384,10,256]{2,0,1:T(8,128)(2,1)} %param.5) | copy-start | bytes 5898244
  1.4 3.0 %copy-start.1 = (f32[10,3,32,256]{3,2,1,0:T(8,128)S(1)}, f32[10,3,32,256]{3,2,1,0:T(8,128)}, u32[]{:S(2)}) copy-start(f32[10,3,32,256]{3,2,1,0:T(8,128)} %init_ref.1) | copy-start | bytes 2949124
